TPU v7x, 32 devices: a whole 2x2x4 slice. The times are simulated.
32 devices in a mesh: band: 8 (over z, x), seg: 4 (over y, core).
Axes of the slice: x: 2, y: 2, z: 4, core: 2. Of those that a mesh axis runs over, the one named last changes fastest.
Arguments:
- voltages: float32 [4, 1, 2, 2, 256, 3072], P('seg', None, None, None, 'band'), may hold values from -6 to 6
- chirp_phase: float32 [1, 256, 4096], P(None, 'seg', 'band'), may hold values from -3.140625 to 3.140625
Outputs:
- dedispersed: float32 [4, 1, 2, 2, 256, 3072], P('seg', None, None, None, 'band')
All inputs are finite; a program needn't handle non-finite values.
Results may differ from a plain program's by a relative error of at most 0.00015.
Values sent between devices are 32-bit elements; how exact they have to be, the bound alone decides.
A program may use at most 64 MiB of HBM per device.

v0:
```python
import functools
import math

import jax
import jax.numpy as jnp
import numpy as np
from jax import lax
from jax.experimental import pallas as pl
from jax.experimental.pallas import tpu as pltpu
from jax.sharding import PartitionSpec as P

LANES = 128
SUBLANES = 8
VMEM_LIMIT = 56 * 1024 * 1024


def split_table(table):
    high = table.astype(jnp.bfloat16)
    low = (table - high.astype(np.float64)).astype(jnp.bfloat16)
    return high, low


def lane_table(direction):
    places = np.arange(LANES)
    angles = direction * 2.0 * np.pi / LANES * (places[:, None] * places[None, :] % LANES)
    cosine, sine = np.cos(angles), np.sin(angles)
    return split_table(np.block([[cosine, sine], [-sine, cosine]]))


def row_table(rows):
    places = np.arange(rows)
    angles = 2.0 * np.pi / rows * (places[:, None] * places[None, :] % rows)
    return split_table(np.concatenate([np.cos(angles), np.sin(angles)], axis=1))


def phase_table(product, length, direction, scale=1.0):
    angles = direction * 2.0 * np.pi / length * (product % length)
    return (np.stack([np.cos(angles), np.sin(angles)]) * scale).astype(np.float32)


def halves(value):
    high = value.astype(jnp.bfloat16)
    return high, (value - high.astype(jnp.float32)).astype(jnp.bfloat16)


def dot(left, right):
    return jnp.dot(left, right, preferred_element_type=jnp.float32)


def transform_list(pairs, direction):
    count = len(pairs)
    if count == 1:
        return pairs
    even = transform_list(pairs[0::2], direction)
    odd = transform_list(pairs[1::2], direction)
    first, second = [], []
    for k in range(count // 2):
        er, ei = even[k]
        pr, pi = odd[k]
        if k == 0:
            tr, ti = pr, pi
        elif 4 * k == count:
            tr, ti = (-pi, pr) if direction > 0 else (pi, -pr)
        else:
            c = math.cos(2.0 * math.pi * k / count)
            s = direction * math.sin(2.0 * math.pi * k / count)
            if 8 * k == count:
                tr, ti = (pr - direction * pi) * c, (pi + direction * pr) * c
            else:
                tr, ti = pr * c - pi * s, pr * s + pi * c
        first.append((er + tr, ei + ti))
        second.append((er - tr, ei - ti))
    return first + second


def forward_kernel(blocks, hist_ref, new_ref, inner_ref, outer_ref, high_ref, low_ref, out_ref):
    hist_blocks = hist_ref.shape[-1] // LANES
    pairs = []
    for j in range(blocks):
        if j < hist_blocks:
            cut = pl.ds(j * LANES, LANES)
            pairs.append((hist_ref[0, 0, 0, :, cut], hist_ref[0, 0, 1, :, cut]))
        else:
            cut = pl.ds((j - hist_blocks) * LANES, LANES)
            pairs.append((new_ref[0, 0, 0, 0, :, cut], new_ref[0, 0, 0, 1, :, cut]))
    lines = []
    for k, (real, imag) in enumerate(transform_list(pairs, -1.0)):
        cosine, sine = inner_ref[0, k : k + 1, :], inner_ref[1, k : k + 1, :]
        lines.append(
            jnp.concatenate([real * cosine - imag * sine, real * sine + imag * cosine], axis=1)
        )
    high, low = halves(jnp.concatenate(lines, axis=0))
    weights = high_ref[...]
    result = dot(high, weights) + dot(low, weights) + dot(high, low_ref[...])
    real, imag = result[:, :LANES], result[:, LANES:]
    cosine = outer_ref[0].reshape(real.shape)
    sine = outer_ref[1].reshape(real.shape)
    place = (out_ref.shape[0],) + out_ref.shape[2:]
    out_ref[:, 0] = (real * cosine - imag * sine).reshape(place)
    out_ref[:, 1] = (real * sine + imag * cosine).reshape(place)


def middle_kernel(in_ref, cos_ref, sin_ref, high_ref, low_ref, out_ref):
    bands, rows_dev = in_ref.shape[0], in_ref.shape[3]
    rows = bands * rows_dev
    high_table, low_table = high_ref[...], low_ref[...]

    def product(top, bottom):
        high, low = halves(jnp.concatenate([top, bottom], axis=0))
        return dot(high_table, high) + dot(high_table, low) + dot(low_table, high)

    real = in_ref[:, 0, 0].reshape(rows, LANES)
    imag = in_ref[:, 1, 0].reshape(rows, LANES)
    spectrum = product(
        jnp.concatenate([real, imag], axis=1), jnp.concatenate([imag, -real], axis=1)
    )
    real, imag = spectrum[:, :LANES], spectrum[:, LANES:]
    cosine, sine = cos_ref[0], sin_ref[0]
    real, imag = real * cosine - imag * sine, real * sine + imag * cosine
    restored = product(
        jnp.concatenate([real, imag], axis=1), jnp.concatenate([-imag, real], axis=1)
    )
    out_ref[:, 0, 0] = restored[:, :LANES].reshape(bands, rows_dev, LANES)
    out_ref[:, 1, 0] = restored[:, LANES:].reshape(bands, rows_dev, LANES)


def backward_kernel(blocks, in_ref, inner_ref, outer_ref, high_ref, low_ref, *rest):
    out_ref = rest[-1]
    lines = blocks * SUBLANES
    skipped = blocks - out_ref.shape[-1] // LANES
    real = in_ref[:, 0].reshape(lines, LANES)
    imag = in_ref[:, 1].reshape(lines, LANES)
    cosine = outer_ref[0].reshape(lines, LANES)
    sine = outer_ref[1].reshape(lines, LANES)
    high, low = halves(
        jnp.concatenate([real * cosine + imag * sine, imag * cosine - real * sine], axis=1)
    )
    weights = high_ref[...]
    result = dot(high, weights) + dot(low, weights) + dot(high, low_ref[...])
    pairs = []
    for k in range(blocks):
        cosine, sine = inner_ref[0, k : k + 1, :], inner_ref[1, k : k + 1, :]
        real = result[k * SUBLANES : (k + 1) * SUBLANES, :LANES]
        imag = result[k * SUBLANES : (k + 1) * SUBLANES, LANES:]
        pairs.append((real * cosine - imag * sine, real * sine + imag * cosine))
    restored = transform_list(pairs, 1.0)
    for j in range(skipped, blocks):
        cut = pl.ds((j - skipped) * LANES, LANES)
        out_ref[0, 0, 0, 0, :, cut] = restored[j][0]
        out_ref[0, 0, 0, 1, :, cut] = restored[j][1]


def whole(array):
    return pl.BlockSpec(array.shape, lambda i: (0,) * array.ndim)


def params():
    return pltpu.CompilerParams(vmem_limit_bytes=VMEM_LIMIT)


def per_device(voltages, chirp_phase):
    rows_dev, valid_cols = voltages.shape[4:]
    cols = valid_cols * 4 // 3
    bands = lax.axis_size("band")
    rows = rows_dev * bands
    length = rows * cols
    blocks = cols // LANES
    own_blocks = blocks // bands
    band = lax.axis_index("band")

    hist_cols = cols // 4
    tail = voltages[:, 0, :, :, :, valid_cols - hist_cols :]
    route = [(i - 1, i) for i in range(1, lax.axis_size("seg"))]
    history = lax.ppermute(tail, "seg", route)

    low_freq = np.arange(blocks)[:, None]
    freq = low_freq + blocks * np.arange(LANES)[None, :]
    inner_forward = jnp.asarray(phase_table(low_freq * np.arange(LANES)[None, :], cols, -1.0))
    inner_backward = jnp.asarray(
        phase_table(low_freq * np.arange(LANES)[None, :], cols, 1.0, 1.0 / length)
    )
    rest = jnp.asarray(
        phase_table(freq[:, None, :] * np.arange(rows_dev)[None, :, None], length, -1.0)
    )
    start = jnp.asarray(
        phase_table(freq[None] * (rows_dev * np.arange(bands))[:, None, None], length, -1.0)
    )
    start = lax.dynamic_index_in_dim(start, band, 1, keepdims=False)[:, :, None, :]
    outer = jnp.stack(
        [rest[0] * start[0] - rest[1] * start[1], rest[0] * start[1] + rest[1] * start[0]]
    )
    lane_forward = [jnp.asarray(t) for t in lane_table(-1.0)]
    lane_backward = [jnp.asarray(t) for t in lane_table(1.0)]
    row_tables = [jnp.asarray(t) for t in row_table(rows)]

    steps = rows_dev // SUBLANES
    sent_shape = (bands, 2, own_blocks, rows_dev, LANES)
    sent_spec = pl.BlockSpec(
        (bands, 2, own_blocks, SUBLANES, LANES), lambda i: (0, 0, 0, i, 0)
    )
    outer_spec = pl.BlockSpec((2, blocks, SUBLANES, LANES), lambda i: (0, 0, i, 0))

    def forward(pol):
        return pl.pallas_call(
            functools.partial(forward_kernel, blocks),
            grid=(steps,),
            in_specs=[
                pl.BlockSpec((1, 1, 2, SUBLANES, hist_cols), lambda i: (0, pol, 0, i, 0)),
                pl.BlockSpec(
                    (1, 1, 1, 2, SUBLANES, valid_cols), lambda i: (0, 0, pol, 0, i, 0)
                ),
                whole(inner_forward),
                outer_spec,
                whole(lane_forward[0]),
                whole(lane_forward[1]),
            ],
            out_specs=sent_spec,
            out_shape=jax.ShapeDtypeStruct(sent_shape, jnp.float32),
            compiler_params=params(),
            name="forward",
        )(history, voltages, inner_forward, outer, *lane_forward)

    def middle(received, cosine, sine):
        piece = pl.BlockSpec((bands, 2, 1, rows_dev, LANES), lambda i: (0, 0, i, 0, 0))
        phase = pl.BlockSpec((1, rows, LANES), lambda i: (i, 0, 0))
        return pl.pallas_call(
            middle_kernel,
            grid=(own_blocks,),
            in_specs=[piece, phase, phase, whole(row_tables[0]), whole(row_tables[1])],
            out_specs=piece,
            out_shape=jax.ShapeDtypeStruct(sent_shape, jnp.float32),
            compiler_params=params(),
            name="middle",
        )(received, cosine, sine, *row_tables)

    def backward(received, pol, into):
        extra = [] if into is None else [into]
        return pl.pallas_call(
            functools.partial(backward_kernel, blocks),
            grid=(steps,),
            in_specs=[
                sent_spec,
                whole(inner_backward),
                outer_spec,
                whole(lane_backward[0]),
                whole(lane_backward[1]),
            ]
            + [pl.BlockSpec(memory_space=pl.ANY)] * len(extra),
            out_specs=pl.BlockSpec(
                (1, 1, 1, 2, SUBLANES, valid_cols), lambda i: (0, 0, pol, 0, i, 0)
            ),
            out_shape=jax.ShapeDtypeStruct(voltages.shape, jnp.float32),
            input_output_aliases={5: 0} if extra else {},
            compiler_params=params(),
            name="backward",
        )(received, inner_backward, outer, *lane_backward, *extra)

    def exchange(block):
        return lax.all_to_all(block, "band", split_axis=0, concat_axis=0, tiled=True)

    seg_rows, width = chirp_phase.shape[1:]
    near = width // blocks
    phases = jnp.transpose(chirp_phase[0].reshape(seg_rows, near, blocks), (2, 0, 1))
    phases = exchange(phases.reshape(bands, own_blocks, seg_rows, near))
    phases = jnp.transpose(phases, (1, 2, 0, 3)).reshape(own_blocks, seg_rows, LANES)
    phases = lax.all_gather(phases, "seg", axis=1, tiled=True)
    cosine, sine = jnp.cos(phases), jnp.sin(phases)

    received = [exchange(forward(pol)) for pol in range(2)]
    returned = [exchange(middle(block, cosine, sine)) for block in received]
    result = None
    for pol in range(2):
        result = backward(returned[pol], pol, result)
    return result


def solution(mesh):
    in_specs = (P("seg", None, None, None, "band", None), P(None, "seg", "band"))
    out_specs = P("seg", None, None, None, "band", None)
    return jax.shard_map(
        per_device, mesh=mesh, in_specs=in_specs, out_specs=out_specs, check_vma=False
    )
```

profile of v0, /device:TPU:0, one launch (start us, length us, event | category | flops | bytes accessed | tf_op | source)
XLA Modules:
  0.0 147.2 jit_solution(16689781637456852619)
XLA Ops:
  0.0 0.0 copy-start.5
  0.0 0.0 copy-start.6
  0.0 1.2 slice_bitcast_fusion
  1.2 2.4 %collective-permute-start = (f32[1,2,2,32,1024]{4,3,2,1,0:T(8,128)S(1)}, f32[1,2,2,32,1024]{4,3,2,1,0:T(8,128)S(1)}, u32[]{:S(2)}, u32[]{:S(2)}) collective-permute-start(f32[1,2,2,32,1024]{4,3,2,1,0:T(8,128)S(1)} %slice_bitcast_fusion), channel_id=1, source_target_pairs={{0,1},{1,2},{2,3},{4,5},{5,6},{6,7},{8,9},{9,10},{10,11},{12,13},{... | collective-permute-start | bytes 1572872 | tf_op jit(solution)/shard_map/ppermute | solution.py:174
  3.6 1.0 copy.14
  4.6 0.2 copy.15
  4.8 0.8 reshape.15
  5.6 6.6 %all-to-all-start.1 = ((f32[8,1,4096]{2,1,0:T(1,128)}), f32[8,1,4096]{2,1,0:T(1,128)S(1)}, u32[]{:S(2)}, u32[]{:S(2)}) async-start(f32[8,1,4096]{2,1,0:T(1,128)} %reshape.15), calls=%async_computation.1 | async-start | bytes 262144 | tf_op jit(solution)/shard_map/all_to_all | solution.py:259
  12.2 0.7 dynamic-slice_bitcast_fusion.1
  13.0 0.0 copy-done.5
  13.0 0.0 copy-done.6
  13.0 0.2 multiply_subtract_fusion
  13.2 1.1 pad_maximum_fusion.outer_ref
  14.2 0.0 collective-permute-done.hist_ref
  14.2 0.0 copy-start.4
  14.2 0.8 copy-done.4
  15.0 4.4 %forward.3 = f32[8,2,4,32,128]{4,3,2,1,0:T(8,128)} custom-call(f32[1,2,2,32,1024]{4,3,2,1,0:T(8,128)} %copy-done.4, f32[1,1,2,2,32,3072]{5,4,3,2,1,0:T(8,128)} %new_ref.3, f32[2,32,128]{2,1,0:T(8,128)} %constant.32.clone.inner_ref, f32[2,32,32,128]{3,2,1,0:T(8,128)} %pad_maximum_fusion.outer_ref, bf16[256,256]{1,0:T(8,128)(2,1)} %constant.36.clone.high_ref, ...), custom_call_target="tpu_custom_call" | custom-call | tf_op jit(solution)/shard_map/forward/pallas_call | solution.py:204
  19.4 0.6 all-to-all-done.1
  20.0 5.4 %all-to-all-start.3 = ((f32[8,2,4,32,128]{4,3,2,1,0:T(8,128)}), f32[8,2,4,32,128]{4,3,2,1,0:T(8,128)S(1)}, u32[]{:S(2)}, u32[]{:S(2)}) async-start(f32[8,2,4,32,128]{4,3,2,1,0:T(8,128)} %forward.3), calls=%async_computation.3 | async-start | bytes 2097152 | tf_op jit(solution)/shard_map/all_to_all | solution.py:259
  25.5 4.4 %forward.2 = f32[8,2,4,32,128]{4,3,2,1,0:T(8,128)} custom-call(f32[1,2,2,32,1024]{4,3,2,1,0:T(8,128)} %copy-done.4, f32[1,1,2,2,32,3072]{5,4,3,2,1,0:T(8,128)} %new_ref.3, f32[2,32,128]{2,1,0:T(8,128)} %constant.32.clone.inner_ref, f32[2,32,32,128]{3,2,1,0:T(8,128)} %pad_maximum_fusion.outer_ref, bf16[256,256]{1,0:T(8,128)(2,1)} %constant.36.clone.high_ref, ...), custom_call_target="tpu_custom_call" | custom-call | tf_op jit(solution)/shard_map/forward/pallas_call | solution.py:204
  29.8 23.2 %all-to-all-done.3.in_ref = f32[8,2,4,32,128]{4,3,2,1,0:T(8,128)S(1)} async-done(((f32[8,2,4,32,128]{4,3,2,1,0:T(8,128)}), f32[8,2,4,32,128]{4,3,2,1,0:T(8,128)S(1)}, u32[]{:S(2)}, u32[]{:S(2)}) %all-to-all-start.3) | async-done | bytes 1048608 | tf_op jit(solution)/shard_map/all_to_all | solution.py:259
  53.0 0.0 copy-start
  53.0 3.6 %all-to-all-start = ((f32[8,2,4,32,128]{4,3,2,1,0:T(8,128)}), f32[8,2,4,32,128]{4,3,2,1,0:T(8,128)S(1)}, u32[]{:S(2)}, u32[]{:S(2)}) async-start(f32[8,2,4,32,128]{4,3,2,1,0:T(8,128)} %forward.2), calls=%async_computation | async-start | bytes 2097152 | tf_op jit(solution)/shard_map/all_to_all | solution.py:259
  56.6 0.5 broadcast.4
  57.1 0.9 reduce
  58.0 0.1 reshape.16
  58.1 0.0 copy-done
  58.1 0.1 copy.17
  58.3 7.0 %all_gather.3 = f32[4,256,128]{2,1,0:T(8,128)S(1)} all-gather(f32[4,64,128]{2,1,0:T(8,128)S(1)} %copy.17), channel_id=1, replica_groups=mesh['band'=8,'seg'=4] {'seg'}, dimensions={1}, use_global_device_ids=true | all-gather | bytes 655360 | tf_op jit(solution)/shard_map/all_gather | solution.py:266
  65.3 2.6 %fusion = (f32[4,256,128]{2,1,0:T(8,128)}, f32[4,256,128]{2,1,0:T(8,128)}) fusion(f32[4,256,128]{2,1,0:T(8,128)S(1)} %all_gather.3), kind=kLoop, calls=%fused_computation.6 | loop fusion | bytes 1572864 | tf_op jit(solution)/shard_map/sin | solution.py:267
  67.9 6.4 %middle.3 = f32[8,2,4,32,128]{4,3,2,1,0:T(8,128)} custom-call(f32[8,2,4,32,128]{4,3,2,1,0:T(8,128)} %copy-done, f32[4,256,128]{2,1,0:T(8,128)} %get-tuple-element.8.cos_ref, f32[4,256,128]{2,1,0:T(8,128)} %get-tuple-element.7.sin_ref, bf16[256,512]{1,0:T(8,128)(2,1)} %constant.40.clone.high_ref, bf16[256,512]{1,0:T(8,128)(2,1)} %constant.41.clone.low_ref), custom_call_target="tpu_custom_call" | custom-call | tf_op jit(solution)/shard_map/middle/pallas_call | solution.py:226
  74.3 8.5 %all-to-all-done.in_ref = f32[8,2,4,32,128]{4,3,2,1,0:T(8,128)S(1)} async-done(((f32[8,2,4,32,128]{4,3,2,1,0:T(8,128)}), f32[8,2,4,32,128]{4,3,2,1,0:T(8,128)S(1)}, u32[]{:S(2)}, u32[]{:S(2)}) %all-to-all-start) | async-done | bytes 1048608 | tf_op jit(solution)/shard_map/all_to_all | solution.py:259
  82.8 0.0 copy-start.1
  82.8 3.6 %all-to-all-start.4 = ((f32[8,2,4,32,128]{4,3,2,1,0:T(8,128)}), f32[8,2,4,32,128]{4,3,2,1,0:T(8,128)S(1)}, u32[]{:S(2)}, u32[]{:S(2)}) async-start(f32[8,2,4,32,128]{4,3,2,1,0:T(8,128)} %middle.3), calls=%async_computation.4 | async-start | bytes 2097152 | tf_op jit(solution)/shard_map/all_to_all | solution.py:259
  86.4 0.0 copy-done.1
  86.4 6.4 %middle.2 = f32[8,2,4,32,128]{4,3,2,1,0:T(8,128)} custom-call(f32[8,2,4,32,128]{4,3,2,1,0:T(8,128)} %copy-done.1, f32[4,256,128]{2,1,0:T(8,128)} %get-tuple-element.8.cos_ref, f32[4,256,128]{2,1,0:T(8,128)} %get-tuple-element.7.sin_ref, bf16[256,512]{1,0:T(8,128)(2,1)} %constant.40.clone.high_ref, bf16[256,512]{1,0:T(8,128)(2,1)} %constant.41.clone.low_ref), custom_call_target="tpu_custom_call" | custom-call | tf_op jit(solution)/shard_map/middle/pallas_call | solution.py:226
  92.9 19.5 %all-to-all-done.4.in_ref = f32[8,2,4,32,128]{4,3,2,1,0:T(8,128)S(1)} async-done(((f32[8,2,4,32,128]{4,3,2,1,0:T(8,128)}), f32[8,2,4,32,128]{4,3,2,1,0:T(8,128)S(1)}, u32[]{:S(2)}, u32[]{:S(2)}) %all-to-all-start.4) | async-done | bytes 1048608 | tf_op jit(solution)/shard_map/all_to_all | solution.py:259
  112.4 0.0 copy-start.2
  112.4 3.6 %all-to-all-start.2 = ((f32[8,2,4,32,128]{4,3,2,1,0:T(8,128)}), f32[8,2,4,32,128]{4,3,2,1,0:T(8,128)S(1)}, u32[]{:S(2)}, u32[]{:S(2)}) async-start(f32[8,2,4,32,128]{4,3,2,1,0:T(8,128)} %middle.2), calls=%async_computation.2 | async-start | bytes 2097152 | tf_op jit(solution)/shard_map/all_to_all | solution.py:259
  116.0 0.0 copy-done.2
  116.0 4.2 %backward.2.rest_0_ = f32[1,1,2,2,32,3072]{5,4,3,2,1,0:T(8,128)} custom-call(f32[8,2,4,32,128]{4,3,2,1,0:T(8,128)} %copy-done.2, f32[2,32,128]{2,1,0:T(8,128)} %constant.33.clone.inner_ref, f32[2,32,32,128]{3,2,1,0:T(8,128)} %pad_maximum_fusion.outer_ref, bf16[256,256]{1,0:T(8,128)(2,1)} %constant.38.clone.high_ref, bf16[256,256]{1,0:T(8,128)(2,1)} %constant.39.clone.low_ref), custom_call_target="tpu_custom_call" | custom-call | tf_op jit(solution)/shard_map/backward/pallas_call | solution.py:238
  120.3 21.7 %all-to-all-done.2.in_ref = f32[8,2,4,32,128]{4,3,2,1,0:T(8,128)S(1)} async-done(((f32[8,2,4,32,128]{4,3,2,1,0:T(8,128)}), f32[8,2,4,32,128]{4,3,2,1,0:T(8,128)S(1)}, u32[]{:S(2)}, u32[]{:S(2)}) %all-to-all-start.2) | async-done | bytes 1048608 | tf_op jit(solution)/shard_map/all_to_all | solution.py:259
  142.0 0.0 copy-start.3
  142.0 1.0 copy-done.3
  143.0 4.2 %backward.3 = f32[1,1,2,2,32,3072]{5,4,3,2,1,0:T(8,128)} custom-call(f32[8,2,4,32,128]{4,3,2,1,0:T(8,128)} %copy-done.3, f32[2,32,128]{2,1,0:T(8,128)} %constant.33.clone.inner_ref, f32[2,32,32,128]{3,2,1,0:T(8,128)} %pad_maximum_fusion.outer_ref, bf16[256,256]{1,0:T(8,128)(2,1)} %constant.38.clone.high_ref, ...), custom_call_target="tpu_custom_call", output_to_operand_aliasing={{}: (5, {})} | custom-call | tf_op jit(solution)/shard_map/backward/pallas_call | solution.py:238
  (2 shorter events, 0.0 us)
Async XLA Ops:
  0.0 13.0 %copy-start.5 = (f32[1,32,32,128]{3,2,1,0:T(8,128)S(1)}, f32[1,32,32,128]{3,2,1,0:T(8,128)}, u32[]{:S(2)}) copy-start(f32[1,32,32,128]{3,2,1,0:T(8,128)} %constant.44) | copy-start | bytes 1572868
  0.0 13.0 %copy-start.6 = (f32[1,32,32,128]{3,2,1,0:T(8,128)S(1)}, f32[1,32,32,128]{3,2,1,0:T(8,128)}, u32[]{:S(2)}) copy-start(f32[1,32,32,128]{3,2,1,0:T(8,128)} %constant.43) | copy-start | bytes 1572868
  1.2 13.0 %collective-permute-start = (f32[1,2,2,32,1024]{4,3,2,1,0:T(8,128)S(1)}, f32[1,2,2,32,1024]{4,3,2,1,0:T(8,128)S(1)}, u32[]{:S(2)}, u32[]{:S(2)}) collective-permute-start(f32[1,2,2,32,1024]{4,3,2,1,0:T(8,128)S(1)} %slice_bitcast_fusion), channel_id=1, source_target_pairs={{0,1},{1,2},{2,3},{4,5},{5,6},{6,7},{8,9},{9,10},{10,11},{12,13},{... | collective-permute-start | bytes 1572872 | tf_op jit(solution)/shard_map/ppermute | solution.py:174
  5.6 14.4 %all-to-all-start.1 = ((f32[8,1,4096]{2,1,0:T(1,128)}), f32[8,1,4096]{2,1,0:T(1,128)S(1)}, u32[]{:S(2)}, u32[]{:S(2)}) async-start(f32[8,1,4096]{2,1,0:T(1,128)} %reshape.15), calls=%async_computation.1 | async-start | bytes 262144 | tf_op jit(solution)/shard_map/all_to_all | solution.py:259
  14.2 0.8 copy-start.4
  20.0 33.0 %all-to-all-start.3 = ((f32[8,2,4,32,128]{4,3,2,1,0:T(8,128)}), f32[8,2,4,32,128]{4,3,2,1,0:T(8,128)S(1)}, u32[]{:S(2)}, u32[]{:S(2)}) async-start(f32[8,2,4,32,128]{4,3,2,1,0:T(8,128)} %forward.3), calls=%async_computation.3 | async-start | bytes 2097152 | tf_op jit(solution)/shard_map/all_to_all | solution.py:259
  53.0 5.1 %copy-start = (f32[8,2,4,32,128]{4,3,2,1,0:T(8,128)}, f32[8,2,4,32,128]{4,3,2,1,0:T(8,128)S(1)}, u32[]{:S(2)}) copy-start(f32[8,2,4,32,128]{4,3,2,1,0:T(8,128)S(1)} %all-to-all-done.3.in_ref) | copy-start | bytes 3145732
  53.0 29.8 %all-to-all-start = ((f32[8,2,4,32,128]{4,3,2,1,0:T(8,128)}), f32[8,2,4,32,128]{4,3,2,1,0:T(8,128)S(1)}, u32[]{:S(2)}, u32[]{:S(2)}) async-start(f32[8,2,4,32,128]{4,3,2,1,0:T(8,128)} %forward.2), calls=%async_computation | async-start | bytes 2097152 | tf_op jit(solution)/shard_map/all_to_all | solution.py:259
  82.8 3.6 %copy-start.1 = (f32[8,2,4,32,128]{4,3,2,1,0:T(8,128)}, f32[8,2,4,32,128]{4,3,2,1,0:T(8,128)S(1)}, u32[]{:S(2)}) copy-start(f32[8,2,4,32,128]{4,3,2,1,0:T(8,128)S(1)} %all-to-all-done.in_ref) | copy-start | bytes 3145732
  82.8 29.6 %all-to-all-start.4 = ((f32[8,2,4,32,128]{4,3,2,1,0:T(8,128)}), f32[8,2,4,32,128]{4,3,2,1,0:T(8,128)S(1)}, u32[]{:S(2)}, u32[]{:S(2)}) async-start(f32[8,2,4,32,128]{4,3,2,1,0:T(8,128)} %middle.3), calls=%async_computation.4 | async-start | bytes 2097152 | tf_op jit(solution)/shard_map/all_to_all | solution.py:259
  112.4 3.6 %copy-start.2 = (f32[8,2,4,32,128]{4,3,2,1,0:T(8,128)}, f32[8,2,4,32,128]{4,3,2,1,0:T(8,128)S(1)}, u32[]{:S(2)}) copy-start(f32[8,2,4,32,128]{4,3,2,1,0:T(8,128)S(1)} %all-to-all-done.4.in_ref) | copy-start | bytes 3145732
  112.4 29.6 %all-to-all-start.2 = ((f32[8,2,4,32,128]{4,3,2,1,0:T(8,128)}), f32[8,2,4,32,128]{4,3,2,1,0:T(8,128)S(1)}, u32[]{:S(2)}, u32[]{:S(2)}) async-start(f32[8,2,4,32,128]{4,3,2,1,0:T(8,128)} %middle.2), calls=%async_computation.2 | async-start | bytes 2097152 | tf_op jit(solution)/shard_map/all_to_all | solution.py:259
  142.0 1.0 copy-start.3
where the time goes:
time: 148 us; the launch traced here: 147 us
  waiting for transfers between devices  73.5 us (50%)
  Pallas kernels  30.1 us (20%)
  starting transfers between devices  25.3 us (17%)
  local copies, waits for them, and re-layouts  9.13 us (6%)
  blocking collectives  7.02 us (5%)
  other arithmetic  2.08 us (1%)
    all_to_all x5, waiting for transfers between devices, exchange(): lax.all_to_all(block, 'band', split_axis=0, concat_axis=0, tiled=True)  73.5 us
    all_to_all x5, starting transfers between devices, exchange(): lax.all_to_all(block, 'band', split_axis=0, concat_axis=0, tiled=True)  22.9 us
    pallas_call x2, Pallas kernels, middle(): pl.pallas_call(middle_kernel, grid=(own_blocks,), in_specs=[piece, phase,...  12.8 us
    pallas_call x2, Pallas kernels, forward(): pl.pallas_call(functools.partial(forward_kernel, blocks), grid=(steps,),...  8.79 us
    pallas_call x2, Pallas kernels, backward(): pl.pallas_call(functools.partial(backward_kernel, blocks), grid=(steps,),...  8.46 us
    all_gather x1, blocking collectives, per_device(): phases = lax.all_gather(phases, 'seg', axis=1, tiled=True)  7.02 us
    unnamed x17, local copies, waits for them, and re-layouts  3.79 us
  transfers between devices with their start and end apart: 6, of which 5 were waited for; matrix products, arithmetic and copies ran while one was open for 6% of the time, Pallas kernels for 18%

commit v1 on v0

v1 whole, which is shorter than its diff:
```python
import functools
import math

import jax
import jax.numpy as jnp
import numpy as np
from jax import lax
from jax.experimental import pallas as pl
from jax.experimental.pallas import tpu as pltpu
from jax.sharding import PartitionSpec as P

LANES = 128
SUBLANES = 8
MESH = pl.DeviceIdType.MESH
VMEM_LIMIT = 56 * 1024 * 1024


def split_table(table):
    high = table.astype(jnp.bfloat16)
    low = (table - high.astype(np.float64)).astype(jnp.bfloat16)
    return high, low


def lane_table(direction):
    places = np.arange(LANES)
    angles = direction * 2.0 * np.pi / LANES * (places[:, None] * places[None, :] % LANES)
    cosine, sine = np.cos(angles), np.sin(angles)
    return split_table(np.block([[cosine, sine], [-sine, cosine]]))


def row_table(rows):
    places = np.arange(rows)
    angles = 2.0 * np.pi / rows * (places[:, None] * places[None, :] % rows)
    return split_table(np.concatenate([np.cos(angles), np.sin(angles)], axis=1))


def phase_table(product, length, direction, scale=1.0):
    angles = direction * 2.0 * np.pi / length * (product % length)
    return (np.stack([np.cos(angles), np.sin(angles)]) * scale).astype(np.float32)


def halves(value):
    high = value.astype(jnp.bfloat16)
    return high, (value - high.astype(jnp.float32)).astype(jnp.bfloat16)


def dot(left, right):
    return jnp.dot(left, right, preferred_element_type=jnp.float32)


def transform_list(pairs, direction):
    count = len(pairs)
    if count == 1:
        return pairs
    even = transform_list(pairs[0::2], direction)
    odd = transform_list(pairs[1::2], direction)
    first, second = [], []
    for k in range(count // 2):
        er, ei = even[k]
        pr, pi = odd[k]
        if k == 0:
            tr, ti = pr, pi
        elif 4 * k == count:
            tr, ti = (-pi, pr) if direction > 0 else (pi, -pr)
        else:
            c = math.cos(2.0 * math.pi * k / count)
            s = direction * math.sin(2.0 * math.pi * k / count)
            if 8 * k == count:
                tr, ti = (pr - direction * pi) * c, (pi + direction * pr) * c
            else:
                tr, ti = pr * c - pi * s, pr * s + pi * c
        first.append((er + tr, ei + ti))
        second.append((er - tr, ei - ti))
    return first + second


def split_dot(value, high_table, low_table):
    high, low = halves(value)
    return dot(high, high_table) + dot(low, high_table) + dot(high, low_table)


def forward_tile(blocks, pol, rows, hist_ref, new_ref, inner_ref, outer_ref, high_ref, low_ref, out_ref):
    hist_blocks = hist_ref.shape[-1] // LANES
    pairs = []
    for j in range(blocks):
        if j < hist_blocks:
            cut = pl.ds(j * LANES, LANES)
            pairs.append((hist_ref[0, pol, 0, rows, cut], hist_ref[0, pol, 1, rows, cut]))
        else:
            cut = pl.ds((j - hist_blocks) * LANES, LANES)
            pairs.append((new_ref[0, 0, pol, 0, rows, cut], new_ref[0, 0, pol, 1, rows, cut]))
    lines = []
    for k, (real, imag) in enumerate(transform_list(pairs, -1.0)):
        cosine, sine = inner_ref[0, k : k + 1, :], inner_ref[1, k : k + 1, :]
        lines.append(
            jnp.concatenate([real * cosine - imag * sine, real * sine + imag * cosine], axis=1)
        )
    result = split_dot(jnp.concatenate(lines, axis=0), high_ref[...], low_ref[...])
    real, imag = result[:, :LANES], result[:, LANES:]
    cosine = outer_ref[0, :, rows, :].reshape(real.shape)
    sine = outer_ref[1, :, rows, :].reshape(real.shape)
    bands, own = out_ref.shape[1], out_ref.shape[3]
    place = (bands, own, SUBLANES, LANES)
    out_ref[pol, :, 0, :, rows, :] = (real * cosine - imag * sine).reshape(place)
    out_ref[pol, :, 1, :, rows, :] = (real * sine + imag * cosine).reshape(place)


def middle_block(pol, block, in_ref, cos_ref, sin_ref, high_ref, low_ref, out_ref):
    bands, rows_dev = in_ref.shape[1], in_ref.shape[4]
    rows = bands * rows_dev
    high_table, low_table = high_ref[...], low_ref[...]

    def product(top, bottom):
        high, low = halves(jnp.concatenate([top, bottom], axis=0))
        return dot(high_table, high) + dot(high_table, low) + dot(low_table, high)

    real = in_ref[pol, :, 0, block].reshape(rows, LANES)
    imag = in_ref[pol, :, 1, block].reshape(rows, LANES)
    spectrum = product(
        jnp.concatenate([real, imag], axis=1), jnp.concatenate([imag, -real], axis=1)
    )
    real, imag = spectrum[:, :LANES], spectrum[:, LANES:]
    cosine, sine = cos_ref[block], sin_ref[block]
    real, imag = real * cosine - imag * sine, real * sine + imag * cosine
    restored = product(
        jnp.concatenate([real, imag], axis=1), jnp.concatenate([-imag, real], axis=1)
    )
    out_ref[pol, :, 0, block] = restored[:, :LANES].reshape(bands, rows_dev, LANES)
    out_ref[pol, :, 1, block] = restored[:, LANES:].reshape(bands, rows_dev, LANES)


def backward_tile(blocks, pol, rows, in_ref, inner_ref, outer_ref, high_ref, low_ref, out_ref):
    lines = blocks * SUBLANES
    skipped = blocks - out_ref.shape[-1] // LANES
    real = in_ref[pol, :, 0, :, rows, :].reshape(lines, LANES)
    imag = in_ref[pol, :, 1, :, rows, :].reshape(lines, LANES)
    cosine = outer_ref[0, :, rows, :].reshape(lines, LANES)
    sine = outer_ref[1, :, rows, :].reshape(lines, LANES)
    result = split_dot(
        jnp.concatenate([real * cosine + imag * sine, imag * cosine - real * sine], axis=1),
        high_ref[...],
        low_ref[...],
    )
    pairs = []
    for k in range(blocks):
        cosine, sine = inner_ref[0, k : k + 1, :], inner_ref[1, k : k + 1, :]
        real = result[k * SUBLANES : (k + 1) * SUBLANES, :LANES]
        imag = result[k * SUBLANES : (k + 1) * SUBLANES, LANES:]
        pairs.append((real * cosine - imag * sine, real * sine + imag * cosine))
    restored = transform_list(pairs, 1.0)
    for j in range(skipped, blocks):
        cut = pl.ds((j - skipped) * LANES, LANES)
        out_ref[0, 0, pol, 0, rows, cut] = restored[j][0]
        out_ref[0, 0, pol, 1, rows, cut] = restored[j][1]


def kernel(
    blocks,
    bands,
    segs,
    hist_ref,
    new_ref,
    phase_ref,
    inner_forward_ref,
    inner_backward_ref,
    outer_ref,
    forward_high,
    forward_low,
    backward_high,
    backward_low,
    row_high,
    row_low,
    out_ref,
    spread,
    received,
    restored,
    returned,
    gathered,
    cosines,
    sines,
    data_send,
    data_recv,
    phase_send,
    phase_recv,
):
    band, seg = lax.axis_index("band"), lax.axis_index("seg")
    own_blocks = spread.shape[3]
    rows_dev = spread.shape[4]
    rows = bands * rows_dev
    steps = rows_dev // SUBLANES

    barrier = pltpu.get_barrier_semaphore()
    for d in range(1, bands):
        pl.semaphore_signal(
            barrier, inc=1, device_id={"band": lax.rem(band + d, bands)}, device_id_type=MESH
        )
    for d in range(1, segs):
        pl.semaphore_signal(
            barrier, inc=1, device_id={"seg": lax.rem(seg + d, segs)}, device_id_type=MESH
        )
    pl.semaphore_wait(barrier, bands - 1 + segs - 1)

    def phase_copy(d):
        return pltpu.make_async_remote_copy(
            src_ref=phase_ref,
            dst_ref=gathered.at[seg],
            send_sem=phase_send.at[d],
            recv_sem=phase_recv.at[d],
            device_id={"seg": lax.rem(seg + d, segs)},
            device_id_type=MESH,
        )

    def data_copy(stage, pol, d):
        source, target = ((spread, received), (restored, returned))[stage]
        other = lax.rem(band + d, bands)
        return pltpu.make_async_remote_copy(
            src_ref=source.at[pol, other],
            dst_ref=target.at[pol, band],
            send_sem=data_send.at[stage, pol, d],
            recv_sem=data_recv.at[stage, pol, d],
            device_id={"band": other},
            device_id_type=MESH,
        )

    def send(stage, pol):
        for d in range(1, bands):
            data_copy(stage, pol, d).start()
        source, target = ((spread, received), (restored, returned))[stage]
        target[pol, band] = source[pol, band]

    def arrive(stage, pol):
        for d in range(1, bands):
            data_copy(stage, pol, d).wait_recv()

    for d in range(1, segs):
        phase_copy(d).start()
    gathered[seg] = phase_ref[...]

    def tile(i):
        return pl.ds(pl.multiple_of(i * SUBLANES, SUBLANES), SUBLANES)

    for pol in range(2):

        @pl.loop(0, steps)
        def _(i):
            forward_tile(
                blocks, pol, tile(i), hist_ref, new_ref, inner_forward_ref, outer_ref,
                forward_high, forward_low, spread,
            )

        send(0, pol)

    for d in range(1, segs):
        phase_copy(d).wait_recv()

    @pl.loop(0, own_blocks)
    def _(block):
        phases = gathered[:, block].reshape(rows, LANES)
        cosines[block] = jnp.cos(phases)
        sines[block] = jnp.sin(phases)

    for pol in range(2):
        arrive(0, pol)

        @pl.loop(0, own_blocks)
        def _(block):
            middle_block(pol, block, received, cosines, sines, row_high, row_low, restored)

        send(1, pol)

    for pol in range(2):
        arrive(1, pol)

        @pl.loop(0, steps)
        def _(i):
            backward_tile(
                blocks, pol, tile(i), returned, inner_backward_ref, outer_ref,
                backward_high, backward_low, out_ref,
            )

    for d in range(1, segs):
        phase_copy(d).wait_send()
    for stage in range(2):
        for pol in range(2):
            for d in range(1, bands):
                data_copy(stage, pol, d).wait_send()


def per_device(voltages, chirp_phase):
    rows_dev, valid_cols = voltages.shape[4:]
    cols = valid_cols * 4 // 3
    bands = lax.axis_size("band")
    rows = rows_dev * bands
    length = rows * cols
    blocks = cols // LANES
    own_blocks = blocks // bands
    band = lax.axis_index("band")

    hist_cols = cols // 4
    tail = voltages[:, 0, :, :, :, valid_cols - hist_cols :]
    route = [(i - 1, i) for i in range(1, lax.axis_size("seg"))]
    history = lax.ppermute(tail, "seg", route)

    low_freq = np.arange(blocks)[:, None]
    freq = low_freq + blocks * np.arange(LANES)[None, :]
    inner_forward = jnp.asarray(phase_table(low_freq * np.arange(LANES)[None, :], cols, -1.0))
    inner_backward = jnp.asarray(
        phase_table(low_freq * np.arange(LANES)[None, :], cols, 1.0, 1.0 / length)
    )
    rest = jnp.asarray(
        phase_table(freq[:, None, :] * np.arange(rows_dev)[None, :, None], length, -1.0)
    )
    start = jnp.asarray(
        phase_table(freq[None] * (rows_dev * np.arange(bands))[:, None, None], length, -1.0)
    )
    start = lax.dynamic_index_in_dim(start, band, 1, keepdims=False)[:, :, None, :]
    outer = jnp.stack(
        [rest[0] * start[0] - rest[1] * start[1], rest[0] * start[1] + rest[1] * start[0]]
    )
    lane_forward = [jnp.asarray(t) for t in lane_table(-1.0)]
    lane_backward = [jnp.asarray(t) for t in lane_table(1.0)]
    row_tables = [jnp.asarray(t) for t in row_table(rows)]

    seg_rows, width = chirp_phase.shape[1:]
    near = width // blocks
    phases = jnp.transpose(chirp_phase[0].reshape(seg_rows, near, blocks), (2, 0, 1))
    phases = lax.all_to_all(
        phases.reshape(bands, own_blocks, seg_rows, near),
        "band", split_axis=0, concat_axis=0, tiled=True,
    )
    phases = jnp.transpose(phases, (1, 2, 0, 3)).reshape(own_blocks, seg_rows, LANES)

    segs = lax.axis_size("seg")
    exchanged = pltpu.VMEM((2, bands, 2, own_blocks, rows_dev, LANES), jnp.float32)
    phase_space = pltpu.VMEM((own_blocks, rows, LANES), jnp.float32)
    operands = (
        history, voltages, phases, inner_forward, inner_backward, outer,
        *lane_forward, *lane_backward, *row_tables,
    )
    return pl.pallas_call(
        functools.partial(kernel, blocks, bands, segs),
        in_specs=[pl.BlockSpec(memory_space=pltpu.VMEM)] * len(operands),
        out_specs=pl.BlockSpec(memory_space=pltpu.VMEM),
        out_shape=jax.ShapeDtypeStruct(voltages.shape, jnp.float32),
        scratch_shapes=[exchanged] * 4
        + [
            pltpu.VMEM((segs, own_blocks, seg_rows, LANES), jnp.float32),
            phase_space,
            phase_space,
            pltpu.SemaphoreType.DMA((2, 2, bands)),
            pltpu.SemaphoreType.DMA((2, 2, bands)),
            pltpu.SemaphoreType.DMA((segs,)),
            pltpu.SemaphoreType.DMA((segs,)),
        ],
        compiler_params=pltpu.CompilerParams(
            vmem_limit_bytes=VMEM_LIMIT, collective_id=0, has_side_effects=True
        ),
        name="dedisperse",
    )(*operands)


def solution(mesh):
    in_specs = (P("seg", None, None, None, "band", None), P(None, "seg", "band"))
    out_specs = P("seg", None, None, None, "band", None)
    return jax.shard_map(
        per_device, mesh=mesh, in_specs=in_specs, out_specs=out_specs, check_vma=False
    )
```

time: 148 us -> 125 us (0.84)
  the two profiles are of different devices: /device:TPU:0 before, /device:TPU:15 now
where the time goes in v1:
time: 125 us; the launch traced here: 122 us
  Pallas kernels  104 us (83%)
  local copies, waits for them, and re-layouts  8.83 us (7%)
  starting transfers between devices  6.95 us (6%)
  other arithmetic  2.06 us (2%)
    pallas_call x1, Pallas kernels, per_device(): pl.pallas_call(functools.partial(kernel, blocks, bands, segs), in_specs=[...  104 us
    all_to_all x1, starting transfers between devices, per_device(): lax.all_to_all(phases.reshape(bands, own_blocks, seg_rows, near), 'band',...  5.66 us
    unnamed x10, local copies, waits for them, and re-layouts  5.54 us
  transfers between devices with their start and end apart: 2, of which 1 were waited for; matrix products, arithmetic and copies ran while one was open for 4% of the time, Pallas kernels for 0%

profile of v1, /device:TPU:15, one launch (start us, length us, event | category | flops | bytes accessed | tf_op | source)
XLA Modules:
  0.0 122.3 jit_solution(2618604143240688621)
XLA Ops:
  0.0 0.0 copy-start.1
  0.0 0.0 copy-start.2
  0.0 1.1 copy.13
  1.1 0.2 copy.14
  1.3 0.8 reshape.15
  2.1 5.7 %all-to-all-start = ((f32[8,1,4096]{2,1,0:T(1,128)}), f32[8,1,4096]{2,1,0:T(1,128)S(1)}, u32[]{:S(2)}, u32[]{:S(2)}) async-start(f32[8,1,4096]{2,1,0:T(1,128)} %reshape.15), calls=%async_computation | async-start | bytes 262144 | tf_op jit(solution)/shard_map/all_to_all | solution.py:327
  7.8 1.1 slice_bitcast_fusion
  8.9 1.3 %collective-permute-start = (f32[1,2,2,32,1024]{4,3,2,1,0:T(8,128)S(1)}, f32[1,2,2,32,1024]{4,3,2,1,0:T(8,128)S(1)}, u32[]{:S(2)}, u32[]{:S(2)}) collective-permute-start(f32[1,2,2,32,1024]{4,3,2,1,0:T(8,128)S(1)} %slice_bitcast_fusion), channel_id=1, source_target_pairs={{0,1},{1,2},{2,3},{4,5},{5,6},{6,7},{8,9},{9,10},{10,11},{12,13},{... | collective-permute-start | bytes 1572872 | tf_op jit(solution)/shard_map/ppermute | solution.py:302
  10.2 0.7 dynamic-slice_bitcast_fusion.1
  10.9 0.0 copy-done.1
  10.9 0.0 copy-done.2
  10.9 0.2 multiply_subtract_fusion
  11.1 1.0 pad_maximum_fusion.outer_ref
  12.1 0.2 all-to-all-done
  12.4 0.5 broadcast.4
  12.9 0.9 reduce
  13.7 0.1 reshape.16
  13.9 0.8 copy.16.phase_ref
  14.7 0.0 collective-permute-done.hist_ref
  14.7 0.0 copy-start
  14.7 0.8 copy-done
  15.5 104.1 %dedisperse.1 = f32[1,1,2,2,32,3072]{5,4,3,2,1,0:T(8,128)} custom-call(f32[1,2,2,32,1024]{4,3,2,1,0:T(8,128)} %copy-done, f32[1,1,2,2,32,3072]{5,4,3,2,1,0:T(8,128)} %new_ref.1, f32[4,64,128]{2,1,0:T(8,128)} %copy.16.phase_ref, f32[2,32,128]{2,1,0:T(8,128)} %constant.32.clone.inner_forward_ref, f32[2,32,128]{2,1,0:T(8,128)} %constant.33.clone.inner_backward_ref, ...), custom_call_target="tpu_custom_call" | custom-call | tf_op jit(solution)/shard_map/dedisperse/pallas_call | solution.py:340
  119.6 2.7 %copy.18 = f32[1,1,2,2,32,3072]{5,4,3,2,1,0:T(8,128)} copy(f32[1,1,2,2,32,3072]{5,4,3,2,1,0:T(8,128)} %dedisperse.1) | data formatting | bytes 3145728
  (2 shorter events, 0.0 us)
Async XLA Ops:
  0.0 10.9 %copy-start.1 = (f32[1,32,32,128]{3,2,1,0:T(8,128)S(1)}, f32[1,32,32,128]{3,2,1,0:T(8,128)}, u32[]{:S(2)}) copy-start(f32[1,32,32,128]{3,2,1,0:T(8,128)} %constant.44) | copy-start | bytes 1572868
  0.0 10.9 %copy-start.2 = (f32[1,32,32,128]{3,2,1,0:T(8,128)S(1)}, f32[1,32,32,128]{3,2,1,0:T(8,128)}, u32[]{:S(2)}) copy-start(f32[1,32,32,128]{3,2,1,0:T(8,128)} %constant.43) | copy-start | bytes 1572868
  2.1 10.3 %all-to-all-start = ((f32[8,1,4096]{2,1,0:T(1,128)}), f32[8,1,4096]{2,1,0:T(1,128)S(1)}, u32[]{:S(2)}, u32[]{:S(2)}) async-start(f32[8,1,4096]{2,1,0:T(1,128)} %reshape.15), calls=%async_computation | async-start | bytes 262144 | tf_op jit(solution)/shard_map/all_to_all | solution.py:327
  8.9 5.8 %collective-permute-start = (f32[1,2,2,32,1024]{4,3,2,1,0:T(8,128)S(1)}, f32[1,2,2,32,1024]{4,3,2,1,0:T(8,128)S(1)}, u32[]{:S(2)}, u32[]{:S(2)}) collective-permute-start(f32[1,2,2,32,1024]{4,3,2,1,0:T(8,128)S(1)} %slice_bitcast_fusion), channel_id=1, source_target_pairs={{0,1},{1,2},{2,3},{4,5},{5,6},{6,7},{8,9},{9,10},{10,11},{12,13},{... | collective-permute-start | bytes 1572872 | tf_op jit(solution)/shard_map/ppermute | solution.py:302
  14.7 0.8 copy-start

commit v2 on v1

--- a/solution.py
+++ b/solution.py
@@ -158,9 +158,8 @@
     blocks,
     bands,
     segs,
-    hist_ref,
     new_ref,
-    phase_ref,
+    chirp_ref,
     inner_forward_ref,
     inner_backward_ref,
     outer_ref,
@@ -175,6 +174,9 @@
     received,
     restored,
     returned,
+    hist_ref,
+    chirps,
+    turned,
     gathered,
     cosines,
     sines,
@@ -182,6 +184,10 @@
     data_recv,
     phase_send,
     phase_recv,
+    chirp_send,
+    chirp_recv,
+    hist_send,
+    hist_recv,
 ):
     band, seg = lax.axis_index("band"), lax.axis_index("seg")
     own_blocks = spread.shape[3]
@@ -202,7 +208,7 @@
 
     def phase_copy(d):
         return pltpu.make_async_remote_copy(
-            src_ref=phase_ref,
+            src_ref=gathered.at[seg],
             dst_ref=gathered.at[seg],
             send_sem=phase_send.at[d],
             recv_sem=phase_recv.at[d],
@@ -232,14 +238,52 @@
         for d in range(1, bands):
             data_copy(stage, pol, d).wait_recv()
 
-    for d in range(1, segs):
-        phase_copy(d).start()
-    gathered[seg] = phase_ref[...]
+    hist_cols = hist_ref.shape[-1]
+    near = chirp_ref.shape[1] // own_blocks
+
+    def hist_copy(pol):
+        recent = pl.ds(new_ref.shape[-1] - hist_cols, hist_cols)
+        return pltpu.make_async_remote_copy(
+            src_ref=new_ref.at[0, 0, pol, :, :, recent],
+            dst_ref=hist_ref.at[0, pol],
+            send_sem=hist_send.at[pol],
+            recv_sem=hist_recv.at[pol],
+            device_id={"seg": lax.rem(seg + 1, segs)},
+            device_id_type=MESH,
+        )
+
+    def chirp_copy(d):
+        other = lax.rem(band + d, bands)
+        return pltpu.make_async_remote_copy(
+            src_ref=chirp_ref.at[other],
+            dst_ref=chirps.at[band],
+            send_sem=chirp_send.at[d],
+            recv_sem=chirp_recv.at[d],
+            device_id={"band": other},
+            device_id_type=MESH,
+        )
+
+    @pl.when(seg < segs - 1)
+    def _():
+        for pol in range(2):
+            hist_copy(pol).start()
+
+    for d in range(1, bands):
+        chirp_copy(d).start()
+    chirps[band] = chirp_ref[band]
+
+    @pl.when(seg == 0)
+    def _():
+        hist_ref[...] = jnp.zeros_like(hist_ref)
 
     def tile(i):
         return pl.ds(pl.multiple_of(i * SUBLANES, SUBLANES), SUBLANES)
 
     for pol in range(2):
+
+        @pl.when(seg > 0)
+        def _():
+            hist_copy(pol).wait_recv()
 
         @pl.loop(0, steps)
         def _(i):
@@ -250,6 +294,16 @@
 
         send(0, pol)
 
+    for d in range(1, bands):
+        chirp_copy(d).wait_recv()
+    for block in range(own_blocks):
+        for source in range(bands):
+            turned[block, source * near : (source + 1) * near] = chirps[
+                source, block * near : (block + 1) * near
+            ]
+        gathered[seg, block] = jnp.transpose(turned[block])
+    for d in range(1, segs):
+        phase_copy(d).start()
     for d in range(1, segs):
         phase_copy(d).wait_recv()
 
@@ -278,6 +332,13 @@
                 backward_high, backward_low, out_ref,
             )
 
+    @pl.when(seg < segs - 1)
+    def _():
+        for pol in range(2):
+            hist_copy(pol).wait_send()
+
+    for d in range(1, bands):
+        chirp_copy(d).wait_send()
     for d in range(1, segs):
         phase_copy(d).wait_send()
     for stage in range(2):
@@ -297,9 +358,6 @@
     band = lax.axis_index("band")
 
     hist_cols = cols // 4
-    tail = voltages[:, 0, :, :, :, valid_cols - hist_cols :]
-    route = [(i - 1, i) for i in range(1, lax.axis_size("seg"))]
-    history = lax.ppermute(tail, "seg", route)
 
     low_freq = np.arange(blocks)[:, None]
     freq = low_freq + blocks * np.arange(LANES)[None, :]
@@ -323,18 +381,14 @@
 
     seg_rows, width = chirp_phase.shape[1:]
     near = width // blocks
-    phases = jnp.transpose(chirp_phase[0].reshape(seg_rows, near, blocks), (2, 0, 1))
-    phases = lax.all_to_all(
-        phases.reshape(bands, own_blocks, seg_rows, near),
-        "band", split_axis=0, concat_axis=0, tiled=True,
-    )
-    phases = jnp.transpose(phases, (1, 2, 0, 3)).reshape(own_blocks, seg_rows, LANES)
+    turned = jnp.transpose(chirp_phase[0]).reshape(near, blocks, seg_rows)
+    turned = jnp.transpose(turned, (1, 0, 2)).reshape(bands, own_blocks * near, seg_rows)
 
     segs = lax.axis_size("seg")
     exchanged = pltpu.VMEM((2, bands, 2, own_blocks, rows_dev, LANES), jnp.float32)
     phase_space = pltpu.VMEM((own_blocks, rows, LANES), jnp.float32)
     operands = (
-        history, voltages, phases, inner_forward, inner_backward, outer,
+        voltages, turned, inner_forward, inner_backward, outer,
         *lane_forward, *lane_backward, *row_tables,
     )
     return pl.pallas_call(
@@ -344,6 +398,9 @@
         out_shape=jax.ShapeDtypeStruct(voltages.shape, jnp.float32),
         scratch_shapes=[exchanged] * 4
         + [
+            pltpu.VMEM((1, 2, 2, rows_dev, hist_cols), jnp.float32),
+            pltpu.VMEM((bands, own_blocks * near, seg_rows), jnp.float32),
+            pltpu.VMEM((own_blocks, LANES, seg_rows), jnp.float32),
             pltpu.VMEM((segs, own_blocks, seg_rows, LANES), jnp.float32),
             phase_space,
             phase_space,
@@ -351,6 +408,10 @@
             pltpu.SemaphoreType.DMA((2, 2, bands)),
             pltpu.SemaphoreType.DMA((segs,)),
             pltpu.SemaphoreType.DMA((segs,)),
+            pltpu.SemaphoreType.DMA((bands,)),
+            pltpu.SemaphoreType.DMA((bands,)),
+            pltpu.SemaphoreType.DMA((2,)),
+            pltpu.SemaphoreType.DMA((2,)),
         ],
         compiler_params=pltpu.CompilerParams(
             vmem_limit_bytes=VMEM_LIMIT, collective_id=0, has_side_effects=True

time: 125 us -> 114 us (0.912); the launches traced: 122 us -> 114 us
  starting transfers between devices: 6.95 us -> 0 us
  local copies, waits for them, and re-layouts: 8.83 us -> 5.32 us
  Pallas kernels: 104 us -> 106 us
    all_to_all x1 -> x0, starting transfers between devices: 5.66 us -> none  [per_device(): lax.all_to_all(phases.reshape(bands, own_blocks, seg_rows, near), 'band',...]
    unnamed x10 -> x2, local copies, waits for them, and re-layouts: 5.54 us -> 3.73 us
    pallas_call x1, Pallas kernels: 104 us -> 106 us  [per_device(): pl.pallas_call(functools.partial(kernel, blocks, bands, segs), in_specs=[...]
    ppermute x1 -> x0, starting transfers between devices: 1.29 us -> none  [per_device(): history = lax.ppermute(tail, 'seg', route)]
  transfers between devices with their start and end apart: 2 -> 0, of which waited for: 1 -> 0; matrix products, arithmetic and copies ran while one was open for 4% -> 0% of each run, Pallas kernels for 0% -> 0%
where the time goes in v2:
time: 114 us
  Pallas kernels  106 us (93%)
  local copies, waits for them, and re-layouts  5.32 us (5%)
  other arithmetic  2.4 us (2%)
    pallas_call x1, Pallas kernels, per_device(): pl.pallas_call(functools.partial(kernel, blocks, bands, segs), in_specs=[...  106 us
    unnamed x2, local copies, waits for them, and re-layouts  3.73 us

profile of v2, /device:TPU:15, one launch (start us, length us, event | category | flops | bytes accessed | tf_op | source)
XLA Modules:
  0.0 113.6 jit_solution(9081877112875709066)
XLA Ops:
  0.0 0.7 dynamic-slice_bitcast_fusion.1
  0.7 1.0 copy.14
  1.8 0.9 copy.15
  2.6 1.4 %multiply_subtract_fusion = (f32[1,32,32,128]{3,2,1,0:T(8,128)S(1)}, f32[1,32,32,128]{3,2,1,0:T(8,128)S(1)}) fusion(f32[1,32,32,128]{3,2,1,0:T(8,128)} %constant.44, f32[1,32,32,128]{3,2,1,0:T(8,128)} %constant.43, f32[32,128]{1,0:T(8,128)S(1)} %get-tuple-element.8, f32[32,128]{1,0:T(8,128)S(1)} %get-tuple-element.7), kind=kLoop, calls=%fused_computation.2 | loop fusion | flops 786432 | bytes 2129920 | tf_op jit(solution)/shard_map/sub | solution.py:376
  4.0 1.0 pad_maximum_fusion.outer_ref
  5.0 105.8 %dedisperse.1 = f32[1,1,2,2,32,3072]{5,4,3,2,1,0:T(8,128)} custom-call(f32[1,1,2,2,32,3072]{5,4,3,2,1,0:T(8,128)} %new_ref.1, f32[8,64,64]{2,1,0:T(8,128)} %bitcast.12, f32[2,32,128]{2,1,0:T(8,128)} %constant.32.clone.inner_forward_ref, f32[2,32,128]{2,1,0:T(8,128)} %constant.33.clone.inner_backward_ref, f32[2,32,32,128]{3,2,1,0:T(8,128)} %pad_maximum_fusion.outer_ref, ...), custom_call_target="tpu_custom_call" | custom-call | tf_op jit(solution)/shard_map/dedisperse/pallas_call | solution.py:394
  110.9 2.7 %copy.17 = f32[1,1,2,2,32,3072]{5,4,3,2,1,0:T(8,128)} copy(f32[1,1,2,2,32,3072]{5,4,3,2,1,0:T(8,128)} %dedisperse.1) | data formatting | bytes 3145728

commit v3 on v2

--- a/solution.py
+++ b/solution.py
@@ -216,27 +216,30 @@
             device_id_type=MESH,
         )
 
-    def data_copy(stage, pol, d):
+    def data_copy(stage, pol, half, d):
+        part = pl.ds(half * (rows_dev // 2), rows_dev // 2)
         source, target = ((spread, received), (restored, returned))[stage]
         other = lax.rem(band + d, bands)
         return pltpu.make_async_remote_copy(
-            src_ref=source.at[pol, other],
-            dst_ref=target.at[pol, band],
-            send_sem=data_send.at[stage, pol, d],
-            recv_sem=data_recv.at[stage, pol, d],
+            src_ref=source.at[pol, other, :, :, part],
+            dst_ref=target.at[pol, band, :, :, part],
+            send_sem=data_send.at[stage, pol, half, d],
+            recv_sem=data_recv.at[stage, pol, half, d],
             device_id={"band": other},
             device_id_type=MESH,
         )
 
-    def send(stage, pol):
+    def send(stage, pol, half):
         for d in range(1, bands):
-            data_copy(stage, pol, d).start()
+            data_copy(stage, pol, half, d).start()
+
+    def keep(stage, pol):
         source, target = ((spread, received), (restored, returned))[stage]
         target[pol, band] = source[pol, band]
 
-    def arrive(stage, pol):
+    def arrive(stage, pol, half):
         for d in range(1, bands):
-            data_copy(stage, pol, d).wait_recv()
+            data_copy(stage, pol, half, d).wait_recv()
 
     hist_cols = hist_ref.shape[-1]
     near = chirp_ref.shape[1] // own_blocks
@@ -285,14 +288,17 @@
         def _():
             hist_copy(pol).wait_recv()
 
-        @pl.loop(0, steps)
-        def _(i):
-            forward_tile(
-                blocks, pol, tile(i), hist_ref, new_ref, inner_forward_ref, outer_ref,
-                forward_high, forward_low, spread,
-            )
-
-        send(0, pol)
+        for half in range(2):
+
+            @pl.loop(half * (steps // 2), (half + 1) * (steps // 2))
+            def _(i):
+                forward_tile(
+                    blocks, pol, tile(i), hist_ref, new_ref, inner_forward_ref, outer_ref,
+                    forward_high, forward_low, spread,
+                )
+
+            send(0, pol, half)
+        keep(0, pol)
 
     for d in range(1, bands):
         chirp_copy(d).wait_recv()
@@ -314,23 +320,27 @@
         sines[block] = jnp.sin(phases)
 
     for pol in range(2):
-        arrive(0, pol)
+        for half in range(2):
+            arrive(0, pol, half)
 
         @pl.loop(0, own_blocks)
         def _(block):
             middle_block(pol, block, received, cosines, sines, row_high, row_low, restored)
 
-        send(1, pol)
+        for half in range(2):
+            send(1, pol, half)
+        keep(1, pol)
 
     for pol in range(2):
-        arrive(1, pol)
-
-        @pl.loop(0, steps)
-        def _(i):
-            backward_tile(
-                blocks, pol, tile(i), returned, inner_backward_ref, outer_ref,
-                backward_high, backward_low, out_ref,
-            )
+        for half in range(2):
+            arrive(1, pol, half)
+
+            @pl.loop(half * (steps // 2), (half + 1) * (steps // 2))
+            def _(i):
+                backward_tile(
+                    blocks, pol, tile(i), returned, inner_backward_ref, outer_ref,
+                    backward_high, backward_low, out_ref,
+                )
 
     @pl.when(seg < segs - 1)
     def _():
@@ -343,8 +353,9 @@
         phase_copy(d).wait_send()
     for stage in range(2):
         for pol in range(2):
-            for d in range(1, bands):
-                data_copy(stage, pol, d).wait_send()
+            for half in range(2):
+                for d in range(1, bands):
+                    data_copy(stage, pol, half, d).wait_send()
 
 
 def per_device(voltages, chirp_phase):
@@ -404,8 +415,8 @@
             pltpu.VMEM((segs, own_blocks, seg_rows, LANES), jnp.float32),
             phase_space,
             phase_space,
-            pltpu.SemaphoreType.DMA((2, 2, bands)),
-            pltpu.SemaphoreType.DMA((2, 2, bands)),
+            pltpu.SemaphoreType.DMA((2, 2, 2, bands)),
+            pltpu.SemaphoreType.DMA((2, 2, 2, bands)),
             pltpu.SemaphoreType.DMA((segs,)),
             pltpu.SemaphoreType.DMA((segs,)),
             pltpu.SemaphoreType.DMA((bands,)),

time: 114 us -> 114 us (level)
  no operation moved by 1% of the time
where the time goes in v3:
time: 114 us; the launch traced here: 113 us
  Pallas kernels  106 us (93%)
  local copies, waits for them, and re-layouts  5.32 us (5%)
  other arithmetic  2.4 us (2%)
    pallas_call x1, Pallas kernels, per_device(): pl.pallas_call(functools.partial(kernel, blocks, bands, segs), in_specs=[...  106 us
    unnamed x2, local copies, waits for them, and re-layouts  3.73 us

profile of v3, /device:TPU:15, one launch (start us, length us, event | category | flops | bytes accessed | tf_op | source)
XLA Modules:
  0.0 113.5 jit_solution(14983617013442906134)
XLA Ops:
  0.0 0.7 dynamic-slice_bitcast_fusion.1
  0.7 1.0 copy.14
  1.8 0.9 copy.15
  2.6 1.4 %multiply_subtract_fusion = (f32[1,32,32,128]{3,2,1,0:T(8,128)S(1)}, f32[1,32,32,128]{3,2,1,0:T(8,128)S(1)}) fusion(f32[1,32,32,128]{3,2,1,0:T(8,128)} %constant.44, f32[1,32,32,128]{3,2,1,0:T(8,128)} %constant.43, f32[32,128]{1,0:T(8,128)S(1)} %get-tuple-element.8, f32[32,128]{1,0:T(8,128)S(1)} %get-tuple-element.7), kind=kLoop, calls=%fused_computation.2 | loop fusion | flops 786432 | bytes 2129920 | tf_op jit(solution)/shard_map/sub | solution.py:387
  4.0 1.0 pad_maximum_fusion.outer_ref
  5.0 105.7 %dedisperse.1 = f32[1,1,2,2,32,3072]{5,4,3,2,1,0:T(8,128)} custom-call(f32[1,1,2,2,32,3072]{5,4,3,2,1,0:T(8,128)} %new_ref.1, f32[8,64,64]{2,1,0:T(8,128)} %bitcast.12, f32[2,32,128]{2,1,0:T(8,128)} %constant.32.clone.inner_forward_ref, f32[2,32,128]{2,1,0:T(8,128)} %constant.33.clone.inner_backward_ref, f32[2,32,32,128]{3,2,1,0:T(8,128)} %pad_maximum_fusion.outer_ref, ...), custom_call_target="tpu_custom_call" | custom-call | tf_op jit(solution)/shard_map/dedisperse/pallas_call | solution.py:405
  110.8 2.7 %copy.17 = f32[1,1,2,2,32,3072]{5,4,3,2,1,0:T(8,128)} copy(f32[1,1,2,2,32,3072]{5,4,3,2,1,0:T(8,128)} %dedisperse.1) | data formatting | bytes 3145728
